TPU v7x, 512 devices: a whole 4x8x8 slice. The times are simulated.
512 devices in a mesh: play: 64 (over y_lo, z, core), col: 8 (over y_hi, x).
Axes of the slice: x: 4, y: 8 (y_hi: 2, y_lo: 4; y = y_hi * 4 + y_lo), z: 8, core: 2. Of those that a mesh axis runs over, the one named last changes fastest.
Arguments:
- embeddings: bfloat16 [65536, 1024], P('play', 'col'), may hold values from -1 to 1
- labels: int32 [3, 65536], P(None, 'play'), may hold values from 0 to 1023
Outputs:
- gradient: float32 [65536, 1024], P('play', 'col')
All inputs are finite; a program needn't handle non-finite values.
Results may differ from a plain program's by a relative error of at most 0.0014.
Values may be sent and summed in bfloat16 or wider, within the bound.
A program may use at most 64 MiB of HBM per device.

v0:
```python
import jax
import jax.numpy as jnp
from jax import lax
from jax.sharding import PartitionSpec as P

scale_logit = 2.0
bias_logit = -1.0
loss_scale = 0.125


def from_behind(value, axis, steps):
    count = lax.axis_size(axis)
    pairs = [(source, (source + steps) % count) for source in range(count)]
    return lax.ppermute(value, axis, pairs)


def shards(embeddings, labels):
    own_block = lax.all_gather(embeddings, "col", axis=1, tiled=True)
    block_rows = own_block.shape[0]
    col_count = lax.axis_size("col")
    row_span = block_rows // col_count
    offset = lax.axis_index("col") * row_span
    gradient = jnp.zeros(own_block.shape, jnp.float32)
    moving = embeddings
    positions = offset + jnp.arange(row_span, dtype=jnp.int32)
    for round_idx in range(labels.shape[0]):
        moving = from_behind(embeddings, "play", round_idx + 1)
        partner = lax.all_to_all(moving, "col", split_axis=0, concat_axis=1, tiled=True)
        scores = lax.dot_general(
            own_block, partner, (((1,), (1,)), ((), ())), preferred_element_type=jnp.float32
        )
        target = (labels[round_idx][:, None] == positions[None, :]).astype(jnp.float32)
        slope = (
            loss_scale * scale_logit * (jax.nn.sigmoid(scale_logit * scores + bias_logit) - target)
        ).astype(jnp.bfloat16)
        gradient = gradient + jnp.dot(slope, partner, preferred_element_type=jnp.float32)
        other_part = lax.dot_general(
            slope, own_block, (((0,), (0,)), ((), ())), preferred_element_type=jnp.float32
        )
        returned = from_behind(other_part, "play", -(round_idx + 1))
        current = lax.dynamic_slice_in_dim(gradient, offset, row_span, 0)
        gradient = lax.dynamic_update_slice_in_dim(gradient, current + returned, offset, 0)
    return lax.psum_scatter(gradient, "col", scatter_dimension=1, tiled=True)


def solution(mesh):
    return jax.shard_map(
        shards,
        mesh=mesh,
        in_specs=(P("play", "col"), P(None, "play")),
        out_specs=P("play", "col"),
        check_vma=False,
    )
```

profile of v0, /device:TPU:6, one launch (start us, length us, event | category | flops | bytes accessed | tf_op | source)
XLA Modules:
  0.0 283.8 jit_solution(186632302345755930)
XLA Ops:
  6.5 0.0 all-gather.2.cloned.1.call-start
  6.5 0.7 all-gather.2.cloned.1.call-update
  7.3 1.9 collective-permute-start
  9.2 15.9 %collective-permute-done = bf16[1024,128]{1,0:T(8,128)(2,1)} collective-permute-done((bf16[1024,128]{1,0:T(8,128)(2,1)}, bf16[1024,128]{1,0:T(8,128)(2,1)}, u32[]{:S(2)}, u32[]{:S(2)}) %collective-permute-start) | collective-permute-done | bytes 262176 | tf_op jit(solution)/shard_map/ppermute | solution.py:14
  25.0 7.3 %all-to-all-start = ((bf16[8,128,128]{2,1,0:T(8,128)(2,1)}), bf16[8,128,128]{2,1,0:T(8,128)(2,1)S(1)}, u32[]{:S(2)}, u32[]{:S(2)}) async-start(bf16[8,128,128]{2,1,0:T(8,128)(2,1)} %bitcast), calls=%async_computation | async-start | bytes 524288 | tf_op jit(solution)/shard_map/all_to_all | solution.py:28
  32.4 1.9 collective-permute-start.4
  34.3 14.8 %collective-permute-done.4 = bf16[1024,128]{1,0:T(8,128)(2,1)} collective-permute-done((bf16[1024,128]{1,0:T(8,128)(2,1)}, bf16[1024,128]{1,0:T(8,128)(2,1)}, u32[]{:S(2)}, u32[]{:S(2)}) %collective-permute-start.4) | collective-permute-done | bytes 262176 | tf_op jit(solution)/shard_map/ppermute | solution.py:14
  49.1 0.0 all-to-all-done
  49.1 10.4 %all-to-all-start.2 = ((bf16[8,128,128]{2,1,0:T(8,128)(2,1)}), bf16[8,128,128]{2,1,0:T(8,128)(2,1)S(1)}, u32[]{:S(2)}, u32[]{:S(2)}) async-start(bf16[8,128,128]{2,1,0:T(8,128)(2,1)} %bitcast.8), calls=%async_computation.2 | async-start | bytes 524288 | tf_op jit(solution)/shard_map/all_to_all | solution.py:28
  59.5 2.8 collective-permute-start.2
  62.3 23.2 %collective-permute-done.2 = bf16[1024,128]{1,0:T(8,128)(2,1)} collective-permute-done((bf16[1024,128]{1,0:T(8,128)(2,1)}, bf16[1024,128]{1,0:T(8,128)(2,1)}, u32[]{:S(2)}, u32[]{:S(2)}) %collective-permute-start.2) | collective-permute-done | bytes 262176 | tf_op jit(solution)/shard_map/ppermute | solution.py:14
  85.5 0.0 all-to-all-done.2
  85.5 9.9 %all-to-all-start.1 = ((bf16[8,128,128]{2,1,0:T(8,128)(2,1)}), bf16[8,128,128]{2,1,0:T(8,128)(2,1)S(1)}, u32[]{:S(2)}, u32[]{:S(2)}) async-start(bf16[8,128,128]{2,1,0:T(8,128)(2,1)} %bitcast.4), calls=%async_computation.1 | async-start | bytes 524288 | tf_op jit(solution)/shard_map/all_to_all | solution.py:28
  95.4 0.0 reduce-scatter.2.cloned.1.call-start
  95.4 0.8 fusion.24
  96.2 0.2 copy.3
  96.4 0.2 copy.5
  96.6 7.7 %all-to-all-done.1 = bf16[8,128,128]{2,1,0:T(8,128)(2,1)S(1)} async-done(((bf16[8,128,128]{2,1,0:T(8,128)(2,1)}), bf16[8,128,128]{2,1,0:T(8,128)(2,1)S(1)}, u32[]{:S(2)}, u32[]{:S(2)}) %all-to-all-start.1) | async-done | bytes 262176 | tf_op jit(solution)/shard_map/all_to_all | solution.py:28
  104.3 0.2 copy.4
  104.5 0.0 all-gather.2.cloned.1.call-done
  104.5 0.0 copy-start
  104.6 2.5 fusion.21
  107.0 0.0 copy-done
  107.0 0.5 fusion.26
  107.5 3.9 %collective-permute-start.1 = (f32[128,1024]{1,0:T(8,128)S(1)}, f32[128,1024]{1,0:T(8,128)S(1)}, u32[]{:S(2)}, u32[]{:S(2)}) collective-permute-start(f32[128,1024]{1,0:T(8,128)S(1)} %fusion.26), channel_id=1, source_target_pairs={{0,504},{8,0},{16,8},{24,16},{32,24},{40,32},{48,40},{56,48},{64,5... | collective-permute-start | bytes 1572872 | tf_op jit(solution)/shard_map/ppermute | solution.py:14
  111.5 0.7 fusion.23
  112.2 0.5 fusion.28
  112.7 3.5 %collective-permute-start.5 = (f32[128,1024]{1,0:T(8,128)S(1)}, f32[128,1024]{1,0:T(8,128)S(1)}, u32[]{:S(2)}, u32[]{:S(2)}) collective-permute-start(f32[128,1024]{1,0:T(8,128)S(1)} %fusion.28), channel_id=1, source_target_pairs={{0,488},{8,496},{16,504},{24,0},{32,8},{40,16},{48,24},{56,32},{64... | collective-permute-start | bytes 1572872 | tf_op jit(solution)/shard_map/ppermute | solution.py:14
  116.1 0.7 fusion.22
  116.9 0.5 fusion.27
  117.4 3.2 %collective-permute-start.3 = (f32[128,1024]{1,0:T(8,128)S(1)}, f32[128,1024]{1,0:T(8,128)S(1)}, u32[]{:S(2)}, u32[]{:S(2)}) collective-permute-start(f32[128,1024]{1,0:T(8,128)S(1)} %fusion.27), channel_id=1, source_target_pairs={{0,496},{8,504},{16,0},{24,8},{32,16},{40,24},{48,32},{56,40},{64,... | collective-permute-start | bytes 1572872 | tf_op jit(solution)/shard_map/ppermute | solution.py:14
  120.5 0.7 fusion.25
  121.2 0.0 collective-permute-done.1
  121.2 0.1 add_dynamic-update-slice_fusion.2
  121.3 0.7 convolution_add_fusion.1
  122.1 24.0 %collective-permute-done.3 = f32[128,1024]{1,0:T(8,128)S(1)} collective-permute-done((f32[128,1024]{1,0:T(8,128)S(1)}, f32[128,1024]{1,0:T(8,128)S(1)}, u32[]{:S(2)}, u32[]{:S(2)}) %collective-permute-start.3) | collective-permute-done | bytes 524320 | tf_op jit(solution)/shard_map/ppermute | solution.py:14
  146.1 0.1 add_dynamic-update-slice_fusion.1
  146.1 2.7 convolution_add_fusion
  148.8 0.0 collective-permute-done.5
  148.8 1.9 add_dynamic-update-slice_fusion
  150.8 0.0 reduce-scatter.2.cloned.1.call-update
  150.8 126.1 %reduce-scatter.2.cloned.1.call-done = f32[1024,128]{1,0:T(8,128)} async-done(((f32[1024,1024]{1,0:T(8,128)}), f32[1024,128]{1,0:T(8,128)}) %reduce-scatter.2.cloned.1.call-update) | async-done | bytes 524304 | tf_op jit(solution)/shard_map/reduce_scatter | solution.py:43
  (1 shorter events, 0.0 us)
Async XLA Ops:
  6.5 98.0 %all-gather.2.cloned.1.call-start = ((), (), s32[]{:S(2)}) async-start(), calls=%async_computation.4 | async-start | bytes 2359296 | tf_op jit(solution)/shard_map/all_gather | solution.py:18
  7.3 17.8 %collective-permute-start = (bf16[1024,128]{1,0:T(8,128)(2,1)}, bf16[1024,128]{1,0:T(8,128)(2,1)}, u32[]{:S(2)}, u32[]{:S(2)}) collective-permute-start(bf16[1024,128]{1,0:T(8,128)(2,1)} %param.2), channel_id=1, source_target_pairs={{0,8},{8,16},{16,24},{24,32},{32,40},{40,48},{48,56},{56,64},{64,7... | collective-permute-start | bytes 786440 | tf_op jit(solution)/shard_map/ppermute | solution.py:14
  25.0 24.1 %all-to-all-start = ((bf16[8,128,128]{2,1,0:T(8,128)(2,1)}), bf16[8,128,128]{2,1,0:T(8,128)(2,1)S(1)}, u32[]{:S(2)}, u32[]{:S(2)}) async-start(bf16[8,128,128]{2,1,0:T(8,128)(2,1)} %bitcast), calls=%async_computation | async-start | bytes 524288 | tf_op jit(solution)/shard_map/all_to_all | solution.py:28
  32.4 16.7 %collective-permute-start.4 = (bf16[1024,128]{1,0:T(8,128)(2,1)}, bf16[1024,128]{1,0:T(8,128)(2,1)}, u32[]{:S(2)}, u32[]{:S(2)}) collective-permute-start(bf16[1024,128]{1,0:T(8,128)(2,1)} %param.2), channel_id=1, source_target_pairs={{0,24},{8,32},{16,40},{24,48},{32,56},{40,64},{48,72},{56,80},{64,... | collective-permute-start | bytes 786440 | tf_op jit(solution)/shard_map/ppermute | solution.py:14
  49.1 36.4 %all-to-all-start.2 = ((bf16[8,128,128]{2,1,0:T(8,128)(2,1)}), bf16[8,128,128]{2,1,0:T(8,128)(2,1)S(1)}, u32[]{:S(2)}, u32[]{:S(2)}) async-start(bf16[8,128,128]{2,1,0:T(8,128)(2,1)} %bitcast.8), calls=%async_computation.2 | async-start | bytes 524288 | tf_op jit(solution)/shard_map/all_to_all | solution.py:28
  59.5 25.9 %collective-permute-start.2 = (bf16[1024,128]{1,0:T(8,128)(2,1)}, bf16[1024,128]{1,0:T(8,128)(2,1)}, u32[]{:S(2)}, u32[]{:S(2)}) collective-permute-start(bf16[1024,128]{1,0:T(8,128)(2,1)} %param.2), channel_id=1, source_target_pairs={{0,16},{8,24},{16,32},{24,40},{32,48},{40,56},{48,64},{56,72},{64,... | collective-permute-start | bytes 786440 | tf_op jit(solution)/shard_map/ppermute | solution.py:14
  85.5 18.9 %all-to-all-start.1 = ((bf16[8,128,128]{2,1,0:T(8,128)(2,1)}), bf16[8,128,128]{2,1,0:T(8,128)(2,1)S(1)}, u32[]{:S(2)}, u32[]{:S(2)}) async-start(bf16[8,128,128]{2,1,0:T(8,128)(2,1)} %bitcast.4), calls=%async_computation.1 | async-start | bytes 524288 | tf_op jit(solution)/shard_map/all_to_all | solution.py:28
  95.4 181.6 %reduce-scatter.2.cloned.1.call-start = ((), (), s32[]{:S(2)}) async-start(), calls=%async_computation.5 | async-start | bytes 4718592 | tf_op jit(solution)/shard_map/reduce_scatter | solution.py:43
  104.5 2.5 copy-start
  107.5 13.7 %collective-permute-start.1 = (f32[128,1024]{1,0:T(8,128)S(1)}, f32[128,1024]{1,0:T(8,128)S(1)}, u32[]{:S(2)}, u32[]{:S(2)}) collective-permute-start(f32[128,1024]{1,0:T(8,128)S(1)} %fusion.26), channel_id=1, source_target_pairs={{0,504},{8,0},{16,8},{24,16},{32,24},{40,32},{48,40},{56,48},{64,5... | collective-permute-start | bytes 1572872 | tf_op jit(solution)/shard_map/ppermute | solution.py:14
  112.7 36.2 %collective-permute-start.5 = (f32[128,1024]{1,0:T(8,128)S(1)}, f32[128,1024]{1,0:T(8,128)S(1)}, u32[]{:S(2)}, u32[]{:S(2)}) collective-permute-start(f32[128,1024]{1,0:T(8,128)S(1)} %fusion.28), channel_id=1, source_target_pairs={{0,488},{8,496},{16,504},{24,0},{32,8},{40,16},{48,24},{56,32},{64... | collective-permute-start | bytes 1572872 | tf_op jit(solution)/shard_map/ppermute | solution.py:14
  117.4 28.7 %collective-permute-start.3 = (f32[128,1024]{1,0:T(8,128)S(1)}, f32[128,1024]{1,0:T(8,128)S(1)}, u32[]{:S(2)}, u32[]{:S(2)}) collective-permute-start(f32[128,1024]{1,0:T(8,128)S(1)} %fusion.27), channel_id=1, source_target_pairs={{0,496},{8,504},{16,0},{24,8},{32,16},{40,24},{48,32},{56,40},{64,... | collective-permute-start | bytes 1572872 | tf_op jit(solution)/shard_map/ppermute | solution.py:14
Sparse Core Ops, SparseCore 0:
  10.4 92.7 all-gather.1
  150.9 125.9 reduce-scatter.1
where the time goes:
time: 286 us; the launch traced here: 284 us
  waiting for transfers between devices  212 us (74%)
  starting transfers between devices  44.8 us (16%)
  between operations  13.6 us (5%)
  matrix products  9.4 us (3%)
    reduce_scatter x1, waiting for transfers between devices, shards(): return lax.psum_scatter(gradient, 'col', scatter_dimension=1, tiled=True)  126 us
    ppermute x6, waiting for transfers between devices, from_behind(): return lax.ppermute(value, axis, pairs)  77.8 us
    all_to_all x3, starting transfers between devices, shards(): lax.all_to_all(moving, 'col', split_axis=0, concat_axis=1, tiled=True)  27.7 us
    ppermute x6, starting transfers between devices, from_behind(): return lax.ppermute(value, axis, pairs)  17.2 us
    all_to_all x3, waiting for transfers between devices, shards(): lax.all_to_all(moving, 'col', split_axis=0, concat_axis=1, tiled=True)  7.74 us
  transfers between devices with their start and end apart: 11, of which 6 were waited for; matrix products, arithmetic and copies ran while one was open for 3% of the time, Pallas kernels for 0%

commit v1 on v0

v1 whole, which is shorter than its diff:
```python
import jax
import jax.numpy as jnp
from jax import lax
from jax.experimental import pallas as pl
from jax.experimental.pallas import tpu as pltpu
from jax.sharding import PartitionSpec as P

MESH = pl.DeviceIdType.MESH
OWN = 3
SLOTS = (0, 1, 2, 4, 5, 6)
ROUNDS = 3


def kernel(
    e_ref, lab_ref, out_ref,
    far, q_ref, own, slope, lab_rows, lab_cols, lab_in,
    part, via, last,
    send_sem, local_sem, r_far, r_qa, r_qb, r_own, r_z, r_lab, r_via, r_last, r_out,
):
    play, col = lax.axis_index("play"), lax.axis_index("col")
    x, h = lax.rem(col, 4), col // 4
    c = lax.rem(play, 2)
    line = h * 64 + play

    def along(delta):
        to = lax.rem(line + delta + 128, 128)
        return {"play": lax.rem(to, 64), "col": (to // 64) * 4 + x}

    def beside(delta):
        return {"play": play, "col": h * 4 + lax.rem(x + delta, 4)}

    def half_of(delta):
        return lax.rem(line + delta + 128, 128) // 64

    across = {"play": play, "col": (1 - h) * 4 + x}
    twin = {"play": play + 1 - 2 * c, "col": col}

    barrier = pltpu.get_barrier_semaphore()
    greeted = [along(d) for d in (-3, -2, -1, 1, 2, 3)] + [beside(o) for o in (1, 2, 3)] + [across]
    for device in greeted:
        pl.semaphore_signal(barrier, inc=1, device_id=device, device_id_type=MESH)
    pl.semaphore_wait(barrier, len(greeted))

    sent = []

    def send(src, dst, recv, device):
        copy = pltpu.make_async_remote_copy(
            src_ref=src, dst_ref=dst, send_sem=send_sem.at[len(sent)], recv_sem=recv,
            device_id=device, device_id_type=MESH,
        )
        copy.start()
        sent.append(copy)

    def arrived(dst, recv):
        pltpu.make_async_copy(dst, dst, recv).wait()

    def place(src, dst, index):
        copy = pltpu.make_async_copy(src, dst, local_sem.at[index])
        copy.start()
        return copy

    for j in range(2):
        send(e_ref.at[:, j], far.at[:, j], r_far.at[j], across)
    for o in (2, 1, 3):
        send(e_ref.at[lax.rem(x + o, 4)], q_ref.at[OWN, h, x], r_qa.at[x], beside(o))
    mine_a = place(e_ref.at[x], q_ref.at[OWN, h, x], 0)
    for d in (1, 2, 3):
        send(lab_ref, lab_in.at[d - 1], r_lab.at[d - 1], along(-d))
    for o in (2, 1, 3):
        send(e_ref.at[pl.ds(2 * h, 2)], own.at[h, x], r_own.at[h, x], beside(o))
    own_a = place(e_ref.at[pl.ds(2 * h, 2)], own.at[h, x], 1)

    lab = lab_ref[:, pl.ds(pl.multiple_of(h * 512, 512), 512)]
    lab = jnp.concatenate([lab, jnp.zeros((8 - ROUNDS, 512), jnp.int32)], axis=0).T
    for r in range(ROUNDS):
        lab_rows[r] = jnp.broadcast_to(lab[:, r : r + 1], (512, 128))
    lab_rows[ROUNDS] = lax.broadcasted_iota(jnp.int32, (512, 128), 0) + h * 512
    lab_cols[ROUNDS] = lax.broadcasted_iota(jnp.int32, (8, 256), 1) + x * 256

    def piece(slot, half, index):
        if index == 0:
            return q_ref.at[slot, half]
        return q_ref.at[slot, 1 - half, :, index - 1]

    def spread(index):
        src = piece(OWN, h, index)
        send(src, piece(1, h, index), r_z.at[1, index], along(2))
        send(src, piece(5, h, index), r_z.at[5, index], along(-2))
        slot = 2 + 2 * c
        send(src, piece(slot, h, index), r_z.at[slot, index], twin)

    def relay(index):
        below, above = half_of(-2), half_of(2)
        arrived(piece(1, below, index), r_z.at[1, index])
        arrived(piece(5, above, index), r_z.at[5, index])
        half = jnp.where(c == 1, below, above)
        src, dst = 5 - 4 * c, 6 - 6 * c
        send(piece(src, half, index), piece(dst, half, index), r_z.at[dst, index], along(2 * c - 1))
        dst = 2 * c
        send(piece(1, below, index), piece(dst, below, index), r_z.at[dst, index], twin)
        dst = 4 + 2 * c
        send(piece(5, above, index), piece(dst, above, index), r_z.at[dst, index], twin)

    def quarter(j):
        arrived(far.at[:, j], r_far.at[j])
        for o in (2, 1, 3):
            send(far.at[lax.rem(x + o, 4), j], q_ref.at[OWN, 1 - h, x, j], r_qb.at[x, j], beside(o))
        return place(far.at[x, j], q_ref.at[OWN, 1 - h, x, j], 2 + j)

    def quarter_arrived(j):
        for o in (1, 2, 3):
            peer = lax.rem(x + o, 4)
            arrived(q_ref.at[OWN, 1 - h, peer, j], r_qb.at[peer, j])

    for o in (1, 2, 3):
        peer = lax.rem(x + o, 4)
        arrived(q_ref.at[OWN, h, peer], r_qa.at[peer])
    mine_a.wait()
    spread(0)
    mine_b = quarter(0)
    quarter_arrived(0)
    mine_b.wait()
    spread(1)
    mine_b = quarter(1)
    for o in (2, 1, 3):
        send(far.at[pl.ds(2 * h, 2)], own.at[1 - h, x], r_own.at[1 - h, x], beside(o))
    own_b = place(far.at[pl.ds(2 * h, 2)], own.at[1 - h, x], 4)
    relay(0)
    quarter_arrived(1)
    mine_b.wait()
    spread(2)
    relay(1)
    for d in (1, 2, 3):
        arrived(lab_in.at[d - 1], r_lab.at[d - 1])
        row = lab_in[d - 1, d - 1 : d, pl.ds(pl.multiple_of(x * 256, 256), 256)]
        lab_cols[d - 1] = jnp.broadcast_to(row, (8, 256))
    own_a.wait()
    own_b.wait()
    for o in (1, 2, 3):
        peer = lax.rem(x + o, 4)
        for half in range(2):
            arrived(own.at[half, peer], r_own.at[half, peer])

    def wide(ref, *at):
        return jnp.concatenate(
            [ref[(*at, half, k)].reshape(-1, 128) for half in range(2) for k in range(4)], axis=1
        )

    def pair(slot):
        scores = lax.dot_general(
            wide(own), wide(q_ref, slot), (((1,), (1,)), ((), ())), preferred_element_type=jnp.float32
        )
        below = slot < OWN
        rows = lab_rows[jnp.where(below, OWN - 1 - slot, ROUNDS)]
        cols = lab_cols[jnp.where(below, ROUNDS, slot - OWN - 1)][:1]
        hit = jnp.concatenate([rows, rows], axis=1) == cols
        base = jnp.where(hit, -0.125, 0.125)
        slope[slot] = (0.125 * jnp.tanh(scores - 0.5) + base).astype(jnp.bfloat16)

    def slot_arrived(slot, delta, indices=(0, 1, 2)):
        for index in indices:
            arrived(piece(slot, half_of(delta), index), r_z.at[slot, index])

    def step(i, _):
        slot = jnp.where(i == 0, 4 - 2 * c, 0)
        slot = jnp.where(i == 1, 1, slot)
        slot = jnp.where(i == 2, 5, slot)
        slot = jnp.where(i == 3, 2 - 2 * c, slot)
        slot = jnp.where(i == 4, 6 - 2 * c, slot)
        slot = jnp.where(i == 5, 6 * c, slot)

        @pl.when((i == 0) | (i > 2))
        def _():
            slot_arrived(slot, slot - OWN)

        pair(slot)
        return 0

    relay(2)
    lax.fori_loop(0, 6, step, 0)

    def product(o):
        xd = lax.rem(x + o, 4)
        left = jnp.concatenate([slope[s] for s in SLOTS], axis=1)
        right = jnp.concatenate(
            [
                jnp.concatenate([q_ref[s, half, xd].reshape(256, 128) for half in range(2)], axis=1)
                for s in SLOTS
            ],
            axis=0,
        )
        value = jnp.dot(left, right, preferred_element_type=jnp.float32)
        for half in range(2):
            part[o, half] = value[:, half * 128 : half * 128 + 128].reshape(2, 2, 128, 128)

    product(2)
    for j in range(2):
        send(part.at[2, :, 0, j], via.at[0, j], r_via.at[0, j], beside(1))
        send(part.at[2, :, 1, j], via.at[1, j], r_via.at[1, j], beside(3))
    product(1)
    for j in range(2):
        send(part.at[1, :, 1, j], last.at[0, :, 1, j], r_last.at[0, 1, j], beside(1))
    product(3)
    for j in range(2):
        send(part.at[3, :, 0, j], last.at[1, :, 0, j], r_last.at[1, 0, j], beside(3))
    for j in range(2):
        arrived(via.at[0, j], r_via.at[0, j])
        part[1, :, 0, j] += via[0, j]
        send(part.at[1, :, 0, j], last.at[0, :, 0, j], r_last.at[0, 0, j], beside(1))
        arrived(via.at[1, j], r_via.at[1, j])
        part[3, :, 1, j] += via[1, j]
        send(part.at[3, :, 1, j], last.at[1, :, 1, j], r_last.at[1, 1, j], beside(3))
    product(0)
    for j in range(2):
        for side in range(2):
            arrived(last.at[0, :, side, j], r_last.at[0, side, j])
            arrived(last.at[1, :, side, j], r_last.at[1, side, j])
            part[0, 1 - h, side, j] += last[0, 1 - h, side, j] + last[1, 1 - h, side, j]
            send(part.at[0, 1 - h, side, j], out_ref.at[2 * h + side, j], r_out.at[side, j], across)
            out_ref[2 * h + side, j] = part[0, h, side, j] + last[0, h, side, j] + last[1, h, side, j]
    for j in range(2):
        for side in range(2):
            arrived(out_ref.at[2 * (1 - h) + side, j], r_out.at[side, j])
    for copy in sent:
        copy.wait_send()


def shards(embeddings, labels):
    bf16, f32, dma = jnp.bfloat16, jnp.float32, pltpu.SemaphoreType.DMA
    out = pl.pallas_call(
        kernel,
        out_shape=jax.ShapeDtypeStruct((4, 2, 128, 128), f32),
        in_specs=[pl.BlockSpec(memory_space=pltpu.VMEM)] * 2,
        out_specs=pl.BlockSpec(memory_space=pltpu.VMEM),
        scratch_shapes=[
            pltpu.VMEM((4, 2, 128, 128), bf16),
            pltpu.VMEM((7, 2, 4, 2, 128, 128), bf16),
            pltpu.VMEM((2, 4, 2, 2, 128, 128), bf16),
            pltpu.VMEM((7, 512, 256), bf16),
            pltpu.VMEM((ROUNDS + 1, 512, 128), jnp.int32),
            pltpu.VMEM((ROUNDS + 1, 8, 256), jnp.int32),
            pltpu.VMEM((ROUNDS, ROUNDS, 1024), jnp.int32),
            pltpu.VMEM((4, 2, 2, 2, 128, 128), f32),
            pltpu.VMEM((2, 2, 2, 128, 128), f32),
            pltpu.VMEM((2, 2, 2, 2, 128, 128), f32),
            dma((64,)), dma((5,)), dma((2,)), dma((4,)), dma((4, 2)), dma((2, 4)), dma((7, 3)),
            dma((3,)), dma((2, 2)), dma((2, 2, 2)), dma((2, 2)),
        ],
        compiler_params=pltpu.CompilerParams(
            collective_id=0, has_side_effects=True, vmem_limit_bytes=40 * 2**20
        ),
    )(embeddings.reshape(4, 2, 128, 128), labels)
    return out.reshape(1024, 128)


def solution(mesh):
    return jax.shard_map(
        shards,
        mesh=mesh,
        in_specs=(P("play", "col"), P(None, "play")),
        out_specs=P("play", "col"),
        check_vma=False,
    )
```

time: 286 us -> 80.4 us (0.28)
  waiting for transfers between devices: 212 us -> 0 us
  Pallas kernels: 0 us -> 76.5 us
  starting transfers between devices: 44.8 us -> 0 us
  between operations: 13.6 us -> 0.01 us
  matrix products: 9.4 us -> 0 us
    reduce_scatter x1 -> x0, waiting for transfers between devices: 126 us -> none  [shards(): return lax.psum_scatter(gradient, 'col', scatter_dimension=1, tiled=True)]
    ppermute x6 -> x0, waiting for transfers between devices: 77.8 us -> none  [from_behind(): return lax.ppermute(value, axis, pairs)]
    pallas_call x0 -> x1, Pallas kernels: none -> 76.5 us  [shards(): pl.pallas_call(kernel, out_shape=jax.ShapeDtypeStruct((4, 2, 128, 128), f...]
    all_to_all x3 -> x0, starting transfers between devices: 27.7 us -> none  [shards(): lax.all_to_all(moving, 'col', split_axis=0, concat_axis=1, tiled=True)]
    ppermute x6 -> x0, starting transfers between devices: 17.2 us -> none  [from_behind(): return lax.ppermute(value, axis, pairs)]
    dot_general x9 -> x0, matrix products: 9.4 us -> none  [the longest x3 4.09 us: shards(): jnp.dot(slope, partner, preferred_element_type=jnp.float32)]
    all_to_all x3 -> x0, waiting for transfers between devices: 7.74 us -> none  [shards(): lax.all_to_all(moving, 'col', split_axis=0, concat_axis=1, tiled=True)]
  transfers between devices with their start and end apart: 11 -> 0, of which waited for: 6 -> 0; matrix products, arithmetic and copies ran while one was open for 3% -> 0% of each run, Pallas kernels for 0% -> 0%
where the time goes in v1:
time: 80.4 us; the launch traced here: 79 us
  Pallas kernels  76.5 us (95%)
  local copies, waits for them, and re-layouts  2.46 us (3%)
    pallas_call x1, Pallas kernels, shards(): pl.pallas_call(kernel, out_shape=jax.ShapeDtypeStruct((4, 2, 128, 128), f...  76.5 us
    unnamed x5, local copies, waits for them, and re-layouts  2.46 us

profile of v1, /device:TPU:6, one launch (start us, length us, event | category | flops | bytes accessed | tf_op | source)
XLA Modules:
  0.0 79.0 jit_solution(9269987132402955056)
XLA Ops:
  0.0 0.0 copy-start
  0.0 0.9 %copy-done = bf16[1024,128]{1,0:T(8,128)(2,1)S(1)} copy-done((bf16[1024,128]{1,0:T(8,128)(2,1)S(1)}, bf16[1024,128]{1,0:T(8,128)(2,1)}, u32[]{:S(2)}) %copy-start) | copy-done | bytes 262168
  1.0 0.0 copy-start.1
  1.0 0.7 copy-done.1
  1.7 76.5 %shard_map.28 = f32[4,2,128,128]{3,2,1,0:T(8,128)S(1)} custom-call(bf16[4,2,128,128]{3,2,1,0:T(8,128)(2,1)S(1)} %bitcast.3, s32[3,1024]{1,0:T(4,128)S(1)} %copy-done.1), custom_call_target="tpu_custom_call" | custom-call | tf_op jit(solution)/shard_map/pallas_call | solution.py:230
  78.2 0.8 %copy.4 = f32[1024,128]{1,0:T(8,128)} copy(f32[1024,128]{1,0:T(8,128)S(1)} %bitcast.2) | data formatting | bytes 1048576
Async XLA Ops:
  0.0 0.9 %copy-start = (bf16[1024,128]{1,0:T(8,128)(2,1)S(1)}, bf16[1024,128]{1,0:T(8,128)(2,1)}, u32[]{:S(2)}) copy-start(bf16[1024,128]{1,0:T(8,128)(2,1)} %param.2) | copy-start | bytes 786436
  1.0 0.7 copy-start.1

commit v2 on v1

v2 whole, which is shorter than its diff:
```python
import jax
import jax.numpy as jnp
from jax import lax
from jax.experimental import pallas as pl
from jax.experimental.pallas import tpu as pltpu
from jax.sharding import PartitionSpec as P

MESH = pl.DeviceIdType.MESH
OWN = 3
SLOTS = (0, 1, 2, 4, 5, 6)
ROUNDS = 3
PARTS = 4
ROWS = 256 // PARTS
FULL = (1, 3)


def kernel(
    e_hbm, lab_hbm, out_ref,
    e_ref, lab_ref, far, hop, q_ref, own, slope, lab_rows, lab_cols, lab_in,
    part, small, got, got_small,
    send_sem, local_sem, r_far, r_qa, r_qb, r_own, r_ob, r_z, r_hop, r_lab, r_got, r_small, r_out,
):
    play, col = lax.axis_index("play"), lax.axis_index("col")
    x, h = lax.rem(col, 4), col // 4
    c = lax.rem(play, 2)
    line = h * 64 + play

    def along(delta):
        to = lax.rem(line + delta + 128, 128)
        return {"play": lax.rem(to, 64), "col": (to // 64) * 4 + x}

    def beside(delta):
        return {"play": play, "col": h * 4 + lax.rem(x + delta, 4)}

    def half_of(delta):
        return lax.rem(line + delta + 128, 128) // 64

    across = {"play": play, "col": (1 - h) * 4 + x}
    twin = {"play": play + 1 - 2 * c, "col": col}

    barrier = pltpu.get_barrier_semaphore()
    greeted = [along(d) for d in (-3, -2, -1, 1, 2, 3)] + [beside(o) for o in (1, 2, 3)] + [across]
    for device in greeted:
        pl.semaphore_signal(barrier, inc=1, device_id=device, device_id_type=MESH)

    z = lax.rem(play // 2, 8)
    edge = (z == 0) | (z == 7)
    other_end = along(jnp.where(z == 0, 14, -14))
    onward = jnp.where(z == 0, 16, -16)

    @pl.when(edge)
    def _():
        for device in (other_end, along(16), along(-16)):
            pl.semaphore_signal(barrier, inc=1, device_id=device, device_id_type=MESH)

    sent = []

    def send(src, dst, recv, device):
        copy = pltpu.make_async_remote_copy(
            src_ref=src, dst_ref=dst, send_sem=send_sem.at[len(sent)], recv_sem=recv,
            device_id=device, device_id_type=MESH,
        )
        copy.start()
        sent.append(copy)

    def arrived(dst, recv):
        pltpu.make_async_copy(dst, dst, recv).wait()

    def place(src, dst, index):
        copy = pltpu.make_async_copy(src, dst, local_sem.at[index])
        copy.start()
        return copy

    fetch_lab = place(lab_hbm, lab_ref, 0)
    fetch_e = place(e_hbm, e_ref, 1)
    fetch_lab.wait()

    lab = lab_ref[:, pl.ds(pl.multiple_of(h * 512, 512), 512)]
    lab = jnp.concatenate([lab, jnp.zeros((8 - ROUNDS, 512), jnp.int32)], axis=0).T
    for r in range(ROUNDS):
        lab_rows[r] = jnp.broadcast_to(lab[:, r : r + 1], (512, 128))
    lab_rows[ROUNDS] = lax.broadcasted_iota(jnp.int32, (512, 128), 0) + h * 512
    lab_cols[ROUNDS] = lax.broadcasted_iota(jnp.int32, (8, 256), 1) + x * 256
    fetch_e.wait()
    pl.semaphore_wait(barrier, jnp.where(edge, len(greeted) + 3, len(greeted)))

    for j in range(PARTS):
        send(e_ref.at[:, j], far.at[:, j], r_far.at[j], across)
    for o in (2, 1, 3):
        send(e_ref.at[lax.rem(x + o, 4)], q_ref.at[OWN, h, x], r_qa.at[x], beside(o))
    mine_a = place(e_ref.at[x], q_ref.at[OWN, h, x], 0)
    for d in (1, 2, 3):
        send(lab_ref, lab_in.at[d - 1], r_lab.at[d - 1], along(-d))
    for o in (2, 1, 3):
        send(e_ref.at[pl.ds(2 * h, 2)], own.at[h, x], r_own.at[x], beside(o))
    own_a = place(e_ref.at[pl.ds(2 * h, 2)], own.at[h, x], 1)

    def piece(slot, half, index):
        if index == 0:
            return q_ref.at[slot, half]
        return q_ref.at[slot, 1 - half, :, index - 1]

    def leave(way):
        slot = jnp.where(z == 0, 1, 5)
        src, dst, recv, device = (
            (piece(OWN, h, 0), piece(1, h, 0), r_z.at[1, 0], along(2)),
            (piece(OWN, h, 0), piece(5, h, 0), r_z.at[5, 0], along(-2)),
            (piece(OWN, h, 0), hop, r_hop.at[0], other_end),
            (hop, piece(slot, h, 0), r_z.at[slot, 0], along(onward)),
        )[way]
        return pltpu.make_async_remote_copy(
            src_ref=src, dst_ref=dst, send_sem=send_sem.at[124 + way], recv_sem=recv,
            device_id=device, device_id_type=MESH,
        )

    def spread(index):
        src = piece(OWN, h, index)
        if index == 0:
            for copy, inside in (leave(0), z != 7), (leave(1), z != 0), (leave(2), edge):
                pl.when(inside)(copy.start)
        else:
            send(src, piece(1, h, index), r_z.at[1, index], along(2))
            send(src, piece(5, h, index), r_z.at[5, index], along(-2))
        slot = 2 + 2 * c
        send(src, piece(slot, h, index), r_z.at[slot, index], twin)

    def relay(index):
        below, above = half_of(-2), half_of(2)
        arrived(piece(1, below, index), r_z.at[1, index])
        arrived(piece(5, above, index), r_z.at[5, index])
        half = jnp.where(c == 1, below, above)
        src, dst = 5 - 4 * c, 6 - 6 * c
        send(piece(src, half, index), piece(dst, half, index), r_z.at[dst, index], along(2 * c - 1))
        dst = 2 * c
        send(piece(1, below, index), piece(dst, below, index), r_z.at[dst, index], twin)
        dst = 4 + 2 * c
        send(piece(5, above, index), piece(dst, above, index), r_z.at[dst, index], twin)

    def fan(j):
        arrived(far.at[:, j], r_far.at[j])
        for o in (2, 1, 3):
            send(far.at[lax.rem(x + o, 4), j], q_ref.at[OWN, 1 - h, x, j], r_qb.at[x, j], beside(o))
        place(far.at[x, j], q_ref.at[OWN, 1 - h, x, j], 2 + j)

    def fan_arrived(j):
        for o in (1, 2, 3):
            peer = lax.rem(x + o, 4)
            arrived(q_ref.at[OWN, 1 - h, peer, j], r_qb.at[peer, j])
        pltpu.make_async_copy(far.at[x, j], q_ref.at[OWN, 1 - h, x, j], local_sem.at[2 + j]).wait()

    for o in (1, 2, 3):
        peer = lax.rem(x + o, 4)
        arrived(q_ref.at[OWN, h, peer], r_qa.at[peer])
    mine_a.wait()
    spread(0)
    fan(0)

    fan(1)
    fan_arrived(0)
    spread(1)
    @pl.when(edge)
    def _():
        leave(2).wait_recv()
        leave(3).start()

    fan(2)
    fan_arrived(1)
    spread(2)
    fan(3)
    for o in (2, 1, 3):
        send(far.at[pl.ds(2 * h, 2)], own.at[1 - h, x], r_ob.at[x], beside(o))
    own_b = place(far.at[pl.ds(2 * h, 2)], own.at[1 - h, x], 2 + PARTS)
    relay(0)
    fan_arrived(2)
    spread(3)
    fan_arrived(3)
    spread(4)
    for index in range(1, PARTS + 1):
        relay(index)
    for d in (1, 2, 3):
        arrived(lab_in.at[d - 1], r_lab.at[d - 1])
        row = lab_in[d - 1, d - 1 : d, pl.ds(pl.multiple_of(x * 256, 256), 256)]
        lab_cols[d - 1] = jnp.broadcast_to(row, (8, 256))
    own_a.wait()
    own_b.wait()
    for o in (1, 2, 3):
        peer = lax.rem(x + o, 4)
        arrived(own.at[h, peer], r_own.at[peer])
        arrived(own.at[1 - h, peer], r_ob.at[peer])

    def wide(ref, *at):
        return jnp.concatenate(
            [ref[(*at, half, k)].reshape(-1, 128) for half in range(2) for k in range(4)], axis=1
        )

    def pair(slot):
        scores = lax.dot_general(
            wide(own), wide(q_ref, slot), (((1,), (1,)), ((), ())), preferred_element_type=jnp.float32
        )
        below = slot < OWN
        rows = lab_rows[jnp.where(below, OWN - 1 - slot, ROUNDS)]
        cols = lab_cols[jnp.where(below, ROUNDS, slot - OWN - 1)][:1]
        hit = jnp.concatenate([rows, rows], axis=1) == cols
        base = jnp.where(hit, -0.125, 0.125)
        slope[slot] = (0.125 * jnp.tanh(scores - 0.5) + base).astype(jnp.bfloat16)

    def slot_arrived(slot, delta, indices=range(PARTS + 1)):
        for index in indices:
            arrived(piece(slot, half_of(delta), index), r_z.at[slot, index])

    def step(i, _):
        slot = jnp.where(i == 0, 4 - 2 * c, 0)
        slot = jnp.where(i == 1, 1, slot)
        slot = jnp.where(i == 2, 5, slot)
        slot = jnp.where(i == 3, 2 - 2 * c, slot)
        slot = jnp.where(i == 4, 6 - 2 * c, slot)
        slot = jnp.where(i == 5, 6 * c, slot)

        @pl.when((i == 0) | (i > 2))
        def _():
            slot_arrived(slot, slot - OWN)

        pair(slot)
        return 0

    lax.fori_loop(0, 6, step, 0)

    def product(o):
        xd = lax.rem(x + o, 4)
        left = jnp.concatenate([slope[s] for s in SLOTS], axis=1)
        right = jnp.concatenate(
            [
                jnp.concatenate([q_ref[s, half, xd].reshape(256, 128) for half in range(2)], axis=1)
                for s in SLOTS
            ],
            axis=0,
        )
        value = jnp.dot(left, right, preferred_element_type=jnp.float32)
        for half in range(2):
            for t in range(4):
                tile = value[t * 128 : t * 128 + 128, half * 128 : half * 128 + 128]
                if o == 0 or (o != 2 and t in FULL):
                    part[o, t, half] = tile
                else:
                    small[o - 1, t, half] = tile.astype(jnp.bfloat16)

    def give(o, t):
        if o != 2 and t in FULL:
            send(part.at[o, t], got.at[o // 2, t // 2], r_got.at[o // 2, t // 2], beside(o))
        else:
            send(small.at[o - 1, t], got_small.at[o - 1, t], r_small.at[o - 1, t], beside(o))

    def finish(t):
        terms = []
        for o in (1, 2, 3):
            if o != 2 and t in FULL:
                arrived(got.at[o // 2, t // 2], r_got.at[o // 2, t // 2])
                terms.append((got, (o // 2, t // 2)))
            else:
                arrived(got_small.at[o - 1, t], r_small.at[o - 1, t])
                terms.append((got_small, (o - 1, t)))

        def total(half):
            value = part[0, t, half]
            for ref, at in terms:
                value = value + ref[(*at, half)].astype(jnp.float32)
            return value

        part[0, t, 1 - h] = total(1 - h)
        send(part.at[0, t, 1 - h], out_ref.at[h, t], r_out.at[t], across)
        out_ref[h, t] = total(h)

    product(2)
    for t in (0, 1):
        give(2, t)
    product(1)
    give(1, 0)
    product(3)
    give(3, 0)
    for o in (1, 3):
        give(o, 1)
    for t in (2, 3):
        for o in (2, 1, 3):
            give(o, t)
    product(0)
    for t in range(4):
        finish(t)
    for t in range(4):
        arrived(out_ref.at[1 - h, t], r_out.at[t])
    for copy in sent:
        copy.wait_send()
    for copy, inside in (leave(0), z != 7), (leave(1), z != 0), (leave(2), edge), (leave(3), edge):
        pl.when(inside)(copy.wait_send)


def shards(embeddings, labels):
    bf16, f32, dma = jnp.bfloat16, jnp.float32, pltpu.SemaphoreType.DMA
    block = (4, PARTS, ROWS, 128)
    out = pl.pallas_call(
        kernel,
        out_shape=jax.ShapeDtypeStruct((2, 4, 128, 128), f32),
        in_specs=[pl.BlockSpec(memory_space=pl.ANY)] * 2,
        out_specs=pl.BlockSpec(memory_space=pltpu.VMEM),
        scratch_shapes=[
            pltpu.VMEM(block, bf16),
            pltpu.VMEM(labels.shape, jnp.int32),
            pltpu.VMEM(block, bf16),
            pltpu.VMEM(block, bf16),
            pltpu.VMEM((7, 2) + block, bf16),
            pltpu.VMEM((2, 4, 2) + block[1:], bf16),
            pltpu.VMEM((7, 512, 256), bf16),
            pltpu.VMEM((ROUNDS + 1, 512, 128), jnp.int32),
            pltpu.VMEM((ROUNDS + 1, 8, 256), jnp.int32),
            pltpu.VMEM((ROUNDS,) + labels.shape, jnp.int32),
            pltpu.VMEM((4, 4, 2, 128, 128), f32),
            pltpu.VMEM((3, 4, 2, 128, 128), bf16),
            pltpu.VMEM((2, 2, 2, 128, 128), f32),
            pltpu.VMEM((3, 4, 2, 128, 128), bf16),
            dma((128,)), dma((3 + PARTS,)), dma((PARTS,)), dma((4,)), dma((4, PARTS)), dma((4,)),
            dma((4,)), dma((7, PARTS + 1)), dma((1,)), dma((3,)), dma((2, 2)), dma((3, 4)), dma((4,)),
        ],
        compiler_params=pltpu.CompilerParams(
            collective_id=0, has_side_effects=True, vmem_limit_bytes=40 * 2**20
        ),
    )(embeddings.reshape(block), labels)
    return out.reshape(1024, 128)


def solution(mesh):
    return jax.shard_map(
        shards,
        mesh=mesh,
        in_specs=(P("play", "col"), P(None, "play")),
        out_specs=P("play", "col"),
        check_vma=False,
    )
```

time: 80.4 us -> 73 us (0.908); the launches traced: 79 us -> 72.8 us
  Pallas kernels: 76.5 us -> 70.3 us
    pallas_call x1, Pallas kernels: 76.5 us -> 70.3 us  [shards(): pl.pallas_call(kernel, out_shape=jax.ShapeDtypeStruct((2, 4, 128, 128), f...]
where the time goes in v2:
time: 73 us; the launch traced here: 72.8 us
  Pallas kernels  70.3 us (96%)
  local copies, waits for them, and re-layouts  2.46 us (3%)
    pallas_call x1, Pallas kernels, shards(): pl.pallas_call(kernel, out_shape=jax.ShapeDtypeStruct((2, 4, 128, 128), f...  70.3 us
    unnamed x5, local copies, waits for them, and re-layouts  2.46 us

profile of v2, /device:TPU:6, one launch (start us, length us, event | category | flops | bytes accessed | tf_op | source)
XLA Modules:
  0.0 72.8 jit_solution(14722112700664832765)
XLA Ops:
  0.0 0.0 copy-start
  0.0 0.9 %copy-done = bf16[1024,128]{1,0:T(8,128)(2,1)S(1)} copy-done((bf16[1024,128]{1,0:T(8,128)(2,1)S(1)}, bf16[1024,128]{1,0:T(8,128)(2,1)}, u32[]{:S(2)}) %copy-start) | copy-done | bytes 262168
  1.0 0.0 copy-start.1
  1.0 0.7 copy-done.1
  1.7 70.3 %shard_map.28 = f32[2,4,128,128]{3,2,1,0:T(8,128)S(1)} custom-call(bf16[4,4,64,128]{3,2,1,0:T(8,128)(2,1)S(1)} %bitcast.3, s32[3,1024]{1,0:T(4,128)S(1)} %copy-done.1), custom_call_target="tpu_custom_call" | custom-call | tf_op jit(solution)/shard_map/pallas_call | solution.py:299
  72.0 0.8 %copy.4 = f32[1024,128]{1,0:T(8,128)} copy(f32[1024,128]{1,0:T(8,128)S(1)} %bitcast.2) | data formatting | bytes 1048576
Async XLA Ops:
  0.0 0.9 %copy-start = (bf16[1024,128]{1,0:T(8,128)(2,1)S(1)}, bf16[1024,128]{1,0:T(8,128)(2,1)}, u32[]{:S(2)}) copy-start(bf16[1024,128]{1,0:T(8,128)(2,1)} %param.2) | copy-start | bytes 786436
  1.0 0.7 copy-start.1

commit v3 on v2

--- a/solution.py
+++ b/solution.py
@@ -11,14 +11,14 @@
 ROUNDS = 3
 PARTS = 4
 ROWS = 256 // PARTS
-FULL = (1, 3)
+FULL = (3,)
 
 
 def kernel(
     e_hbm, lab_hbm, out_ref,
-    e_ref, lab_ref, far, hop, q_ref, own, slope, lab_rows, lab_cols, lab_in,
+    e_ref, lab_ref, far, hop, q_ref, own, extra, slope, lab_rows, lab_cols, lab_in,
     part, small, got, got_small,
-    send_sem, local_sem, r_far, r_qa, r_qb, r_own, r_ob, r_z, r_hop, r_lab, r_got, r_small, r_out,
+    send_sem, local_sem, r_far, r_qa, r_qb, r_own, r_ob, r_ex, r_z, r_hop, r_lab, r_got, r_small, r_out,
 ):
     play, col = lax.axis_index("play"), lax.axis_index("col")
     x, h = lax.rem(col, 4), col // 4
@@ -75,11 +75,13 @@
     fetch_e = place(e_hbm, e_ref, 1)
     fetch_lab.wait()
 
-    lab = lab_ref[:, pl.ds(pl.multiple_of(h * 512, 512), 512)]
-    lab = jnp.concatenate([lab, jnp.zeros((8 - ROUNDS, 512), jnp.int32)], axis=0).T
-    for r in range(ROUNDS):
-        lab_rows[r] = jnp.broadcast_to(lab[:, r : r + 1], (512, 128))
-    lab_rows[ROUNDS] = lax.broadcasted_iota(jnp.int32, (512, 128), 0) + h * 512
+    other = (1 - h) * 512 + 384
+    for at, size, start in (0, 512, h * 512), (512, 128, other):
+        lab = lab_ref[:, pl.ds(pl.multiple_of(start, 128), size)]
+        lab = jnp.concatenate([lab, jnp.zeros((8 - ROUNDS, size), jnp.int32)], axis=0).T
+        for r in range(ROUNDS):
+            lab_rows[r, at : at + size] = jnp.broadcast_to(lab[:, r : r + 1], (size, 128))
+        lab_rows[ROUNDS, at : at + size] = lax.broadcasted_iota(jnp.int32, (size, 128), 0) + start
     lab_cols[ROUNDS] = lax.broadcasted_iota(jnp.int32, (8, 256), 1) + x * 256
     fetch_e.wait()
     pl.semaphore_wait(barrier, jnp.where(edge, len(greeted) + 3, len(greeted)))
@@ -94,6 +96,10 @@
     for o in (2, 1, 3):
         send(e_ref.at[pl.ds(2 * h, 2)], own.at[h, x], r_own.at[x], beside(o))
     own_a = place(e_ref.at[pl.ds(2 * h, 2)], own.at[h, x], 1)
+    late = (3 - 2 * h, pl.ds(PARTS // 2, PARTS // 2))
+    for o in (2, 1, 3):
+        send(e_ref.at[late], extra.at[h, x], r_ex.at[h, x], beside(o))
+    extra_a = place(e_ref.at[late], extra.at[h, x], 3 + PARTS)
 
     def piece(slot, half, index):
         if index == 0:
@@ -170,6 +176,9 @@
     for o in (2, 1, 3):
         send(far.at[pl.ds(2 * h, 2)], own.at[1 - h, x], r_ob.at[x], beside(o))
     own_b = place(far.at[pl.ds(2 * h, 2)], own.at[1 - h, x], 2 + PARTS)
+    for o in (2, 1, 3):
+        send(far.at[late], extra.at[1 - h, x], r_ex.at[1 - h, x], beside(o))
+    extra_b = place(far.at[late], extra.at[1 - h, x], 4 + PARTS)
     relay(0)
     fan_arrived(2)
     spread(3)
@@ -183,10 +192,14 @@
         lab_cols[d - 1] = jnp.broadcast_to(row, (8, 256))
     own_a.wait()
     own_b.wait()
+    extra_a.wait()
+    extra_b.wait()
     for o in (1, 2, 3):
         peer = lax.rem(x + o, 4)
         arrived(own.at[h, peer], r_own.at[peer])
         arrived(own.at[1 - h, peer], r_ob.at[peer])
+        for half in range(2):
+            arrived(extra.at[half, peer], r_ex.at[half, peer])
 
     def wide(ref, *at):
         return jnp.concatenate(
@@ -195,7 +208,7 @@
 
     def pair(slot):
         scores = lax.dot_general(
-            wide(own), wide(q_ref, slot), (((1,), (1,)), ((), ())), preferred_element_type=jnp.float32
+            jnp.concatenate([wide(own), wide(extra)], axis=0), wide(q_ref, slot), (((1,), (1,)), ((), ())), preferred_element_type=jnp.float32
         )
         below = slot < OWN
         rows = lab_rows[jnp.where(below, OWN - 1 - slot, ROUNDS)]
@@ -230,23 +243,24 @@
         left = jnp.concatenate([slope[s] for s in SLOTS], axis=1)
         right = jnp.concatenate(
             [
-                jnp.concatenate([q_ref[s, half, xd].reshape(256, 128) for half in range(2)], axis=1)
+                jnp.concatenate([q_ref[s, half, xd].reshape(256, 128) for half in (h, 1 - h)], axis=1)
                 for s in SLOTS
             ],
             axis=0,
         )
         value = jnp.dot(left, right, preferred_element_type=jnp.float32)
-        for half in range(2):
-            for t in range(4):
-                tile = value[t * 128 : t * 128 + 128, half * 128 : half * 128 + 128]
+        for t in range(4):
+            for k in range(2):
+                row, column = (t * 128, k * 128) if t < 3 else (384 + k * 128, 0)
+                tile = value[row : row + 128, column : column + 128]
                 if o == 0 or (o != 2 and t in FULL):
-                    part[o, t, half] = tile
+                    part[o, t, k] = tile
                 else:
-                    small[o - 1, t, half] = tile.astype(jnp.bfloat16)
+                    small[o - 1, t, k] = tile.astype(jnp.bfloat16)
 
     def give(o, t):
         if o != 2 and t in FULL:
-            send(part.at[o, t], got.at[o // 2, t // 2], r_got.at[o // 2, t // 2], beside(o))
+            send(part.at[o, t], got.at[o // 2, FULL.index(t)], r_got.at[o // 2, FULL.index(t)], beside(o))
         else:
             send(small.at[o - 1, t], got_small.at[o - 1, t], r_small.at[o - 1, t], beside(o))
 
@@ -254,8 +268,8 @@
         terms = []
         for o in (1, 2, 3):
             if o != 2 and t in FULL:
-                arrived(got.at[o // 2, t // 2], r_got.at[o // 2, t // 2])
-                terms.append((got, (o // 2, t // 2)))
+                arrived(got.at[o // 2, FULL.index(t)], r_got.at[o // 2, FULL.index(t)])
+                terms.append((got, (o // 2, FULL.index(t))))
             else:
                 arrived(got_small.at[o - 1, t], r_small.at[o - 1, t])
                 terms.append((got_small, (o - 1, t)))
@@ -266,9 +280,12 @@
                 value = value + ref[(*at, half)].astype(jnp.float32)
             return value
 
-        part[0, t, 1 - h] = total(1 - h)
-        send(part.at[0, t, 1 - h], out_ref.at[h, t], r_out.at[t], across)
-        out_ref[h, t] = total(h)
+        if t < 3:
+            part[0, t, 1] = total(1)
+            send(part.at[0, t, 1], out_ref.at[h, t], r_out.at[t], across)
+        else:
+            out_ref[1 - h, t] = total(1)
+        out_ref[h, t] = total(0)
 
     product(2)
     for t in (0, 1):
@@ -285,7 +302,7 @@
     product(0)
     for t in range(4):
         finish(t)
-    for t in range(4):
+    for t in range(3):
         arrived(out_ref.at[1 - h, t], r_out.at[t])
     for copy in sent:
         copy.wait_send()
@@ -308,16 +325,17 @@
             pltpu.VMEM(block, bf16),
             pltpu.VMEM((7, 2) + block, bf16),
             pltpu.VMEM((2, 4, 2) + block[1:], bf16),
-            pltpu.VMEM((7, 512, 256), bf16),
-            pltpu.VMEM((ROUNDS + 1, 512, 128), jnp.int32),
+            pltpu.VMEM((2, 4, PARTS // 2) + block[2:], bf16),
+            pltpu.VMEM((7, 640, 256), bf16),
+            pltpu.VMEM((ROUNDS + 1, 640, 128), jnp.int32),
             pltpu.VMEM((ROUNDS + 1, 8, 256), jnp.int32),
             pltpu.VMEM((ROUNDS,) + labels.shape, jnp.int32),
             pltpu.VMEM((4, 4, 2, 128, 128), f32),
             pltpu.VMEM((3, 4, 2, 128, 128), bf16),
-            pltpu.VMEM((2, 2, 2, 128, 128), f32),
+            pltpu.VMEM((2, len(FULL), 2, 128, 128), f32),
             pltpu.VMEM((3, 4, 2, 128, 128), bf16),
-            dma((128,)), dma((3 + PARTS,)), dma((PARTS,)), dma((4,)), dma((4, PARTS)), dma((4,)),
-            dma((4,)), dma((7, PARTS + 1)), dma((1,)), dma((3,)), dma((2, 2)), dma((3, 4)), dma((4,)),
+            dma((128,)), dma((5 + PARTS,)), dma((PARTS,)), dma((4,)), dma((4, PARTS)), dma((4,)),
+            dma((4,)), dma((2, 4)), dma((7, PARTS + 1)), dma((1,)), dma((3,)), dma((2, len(FULL))), dma((3, 4)), dma((3,)),
         ],
         compiler_params=pltpu.CompilerParams(
             collective_id=0, has_side_effects=True, vmem_limit_bytes=40 * 2**20

time: 73 us -> 69.6 us (0.953)
  Pallas kernels: 70.3 us -> 66.4 us
    pallas_call x1, Pallas kernels: 70.3 us -> 66.4 us  [shards(): pl.pallas_call(kernel, out_shape=jax.ShapeDtypeStruct((2, 4, 128, 128), f...]
where the time goes in v3:
time: 69.6 us; the launch traced here: 68.9 us
  Pallas kernels  66.4 us (95%)
  local copies, waits for them, and re-layouts  2.46 us (4%)
    pallas_call x1, Pallas kernels, shards(): pl.pallas_call(kernel, out_shape=jax.ShapeDtypeStruct((2, 4, 128, 128), f...  66.4 us
    unnamed x5, local copies, waits for them, and re-layouts  2.46 us

profile of v3, /device:TPU:6, one launch (start us, length us, event | category | flops | bytes accessed | tf_op | source)
XLA Modules:
  0.0 68.9 jit_solution(7542852212639378932)
XLA Ops:
  0.0 0.0 copy-start
  0.0 0.9 %copy-done = bf16[1024,128]{1,0:T(8,128)(2,1)S(1)} copy-done((bf16[1024,128]{1,0:T(8,128)(2,1)S(1)}, bf16[1024,128]{1,0:T(8,128)(2,1)}, u32[]{:S(2)}) %copy-start) | copy-done | bytes 262168
  1.0 0.0 copy-start.1
  1.0 0.7 %copy-done.1 = s32[3,1024]{1,0:T(4,128)S(1)} copy-done((s32[3,1024]{1,0:T(4,128)S(1)}, s32[3,1024]{1,0:T(4,128)}, u32[]{:S(2)}) %copy-start.1) | copy-done | bytes 12312
  1.7 66.4 %shard_map.28 = f32[2,4,128,128]{3,2,1,0:T(8,128)S(1)} custom-call(bf16[4,4,64,128]{3,2,1,0:T(8,128)(2,1)S(1)} %bitcast.3, s32[3,1024]{1,0:T(4,128)S(1)} %copy-done.1), custom_call_target="tpu_custom_call" | custom-call | tf_op jit(solution)/shard_map/pallas_call | solution.py:316
  68.1 0.8 %copy.4 = f32[1024,128]{1,0:T(8,128)} copy(f32[1024,128]{1,0:T(8,128)S(1)} %bitcast.2) | data formatting | bytes 1048576
Async XLA Ops:
  0.0 0.9 %copy-start = (bf16[1024,128]{1,0:T(8,128)(2,1)S(1)}, bf16[1024,128]{1,0:T(8,128)(2,1)}, u32[]{:S(2)}) copy-start(bf16[1024,128]{1,0:T(8,128)(2,1)} %param.2) | copy-start | bytes 786436
  1.0 0.7 %copy-start.1 = (s32[3,1024]{1,0:T(4,128)S(1)}, s32[3,1024]{1,0:T(4,128)}, u32[]{:S(2)}) copy-start(s32[3,1024]{1,0:T(4,128)} %lab_hbm.1) | copy-start | bytes 36868

commit v4 on v3

--- a/solution.py
+++ b/solution.py
@@ -11,14 +11,14 @@
 ROUNDS = 3
 PARTS = 4
 ROWS = 256 // PARTS
-FULL = (3,)
+PARCELS = ((1, 0, 1), (1, 1, 3), (0, 0, 3))
 
 
 def kernel(
     e_hbm, lab_hbm, out_ref,
     e_ref, lab_ref, far, hop, q_ref, own, extra, slope, lab_rows, lab_cols, lab_in,
     part, small, got, got_small,
-    send_sem, local_sem, r_far, r_qa, r_qb, r_own, r_ob, r_ex, r_z, r_hop, r_lab, r_got, r_small, r_out,
+    send_sem, local_sem, r_far, r_qa, r_qb, r_own, r_ob, r_ex, r_z, r_hop, r_lab, r_small, r_out,
 ):
     play, col = lax.axis_index("play"), lax.axis_index("col")
     x, h = lax.rem(col, 4), col // 4
@@ -160,32 +160,33 @@
     mine_a.wait()
     spread(0)
     fan(0)
-
     fan(1)
     fan_arrived(0)
     spread(1)
+    fan(2)
     @pl.when(edge)
     def _():
         leave(2).wait_recv()
         leave(3).start()
 
-    fan(2)
+    fan(3)
     fan_arrived(1)
     spread(2)
-    fan(3)
     for o in (2, 1, 3):
         send(far.at[pl.ds(2 * h, 2)], own.at[1 - h, x], r_ob.at[x], beside(o))
     own_b = place(far.at[pl.ds(2 * h, 2)], own.at[1 - h, x], 2 + PARTS)
     for o in (2, 1, 3):
         send(far.at[late], extra.at[1 - h, x], r_ex.at[1 - h, x], beside(o))
     extra_b = place(far.at[late], extra.at[1 - h, x], 4 + PARTS)
-    relay(0)
     fan_arrived(2)
     spread(3)
     fan_arrived(3)
     spread(4)
-    for index in range(1, PARTS + 1):
-        relay(index)
+    relay(1)
+    relay(2)
+    relay(0)
+    relay(3)
+    relay(4)
     for d in (1, 2, 3):
         arrived(lab_in.at[d - 1], r_lab.at[d - 1])
         row = lab_in[d - 1, d - 1 : d, pl.ds(pl.multiple_of(x * 256, 256), 256)]
@@ -253,57 +254,67 @@
             for k in range(2):
                 row, column = (t * 128, k * 128) if t < 3 else (384 + k * 128, 0)
                 tile = value[row : row + 128, column : column + 128]
-                if o == 0 or (o != 2 and t in FULL):
+                if o == 0 or (o != 2 and t == 3):
                     part[o, t, k] = tile
                 else:
-                    small[o - 1, t, k] = tile.astype(jnp.bfloat16)
-
-    def give(o, t):
-        if o != 2 and t in FULL:
-            send(part.at[o, t], got.at[o // 2, FULL.index(t)], r_got.at[o // 2, FULL.index(t)], beside(o))
-        else:
-            send(small.at[o - 1, t], got_small.at[o - 1, t], r_small.at[o - 1, t], beside(o))
-
-    def finish(t):
-        terms = []
+                    small[o - 1, k, t] = tile.astype(jnp.bfloat16)
+
+    def parcel(o, m):
+        if m < 3:
+            k, first, end = PARCELS[m]
+            at = (o - 1, k, pl.ds(first, end - first))
+            return small.at[at], got_small.at[at], r_small.at[o - 1, m]
+        if o == 2:
+            return small.at[1, :, 3], got_small.at[1, :, 3], r_small.at[1, 3]
+        return part.at[o, 3], got.at[o // 2], r_small.at[o - 1, 3]
+
+    def give(o, m):
+        send(*parcel(o, m), beside(o))
+
+    def take(m):
         for o in (1, 2, 3):
-            if o != 2 and t in FULL:
-                arrived(got.at[o // 2, FULL.index(t)], r_got.at[o // 2, FULL.index(t)])
-                terms.append((got, (o // 2, FULL.index(t))))
+            _, dst, recv = parcel(o, m)
+            arrived(dst, recv)
+
+    def total(t, k):
+        value = part[0, t, k] + got_small[1, k, t].astype(jnp.float32)
+        if t == 3:
+            return value + got[0, k] + got[1, k]
+        return value + got_small[0, k, t].astype(jnp.float32) + got_small[2, k, t].astype(jnp.float32)
+
+    def finish(m):
+        take(m)
+        if m == 3:
+            out_ref[h, 3] = total(3, 0)
+            out_ref[1 - h, 3] = total(3, 1)
+            return
+        k, first, end = PARCELS[m]
+        for t in range(first, end):
+            if k == 1:
+                part[0, t, 1] = total(t, 1)
             else:
-                arrived(got_small.at[o - 1, t], r_small.at[o - 1, t])
-                terms.append((got_small, (o - 1, t)))
-
-        def total(half):
-            value = part[0, t, half]
-            for ref, at in terms:
-                value = value + ref[(*at, half)].astype(jnp.float32)
-            return value
-
-        if t < 3:
-            part[0, t, 1] = total(1)
-            send(part.at[0, t, 1], out_ref.at[h, t], r_out.at[t], across)
-        else:
-            out_ref[1 - h, t] = total(1)
-        out_ref[h, t] = total(0)
+                out_ref[h, t] = total(t, 0)
+        if k == 1:
+            rows = pl.ds(first, end - first)
+            send(part.at[0, rows, 1], out_ref.at[h, rows], r_out.at[m], across)
 
     product(2)
-    for t in (0, 1):
-        give(2, t)
+    give(2, 0)
     product(1)
     give(1, 0)
+    give(2, 1)
     product(3)
     give(3, 0)
-    for o in (1, 3):
-        give(o, 1)
-    for t in (2, 3):
+    give(1, 1)
+    give(3, 1)
+    for m in (2, 3):
         for o in (2, 1, 3):
-            give(o, t)
+            give(o, m)
     product(0)
-    for t in range(4):
-        finish(t)
-    for t in range(3):
-        arrived(out_ref.at[1 - h, t], r_out.at[t])
+    for m in range(4):
+        finish(m)
+    for k, first, end in PARCELS[:2]:
+        arrived(out_ref.at[1 - h, pl.ds(first, end - first)], r_out.at[first])
     for copy in sent:
         copy.wait_send()
     for copy, inside in (leave(0), z != 7), (leave(1), z != 0), (leave(2), edge), (leave(3), edge):
@@ -331,11 +342,11 @@
             pltpu.VMEM((ROUNDS + 1, 8, 256), jnp.int32),
             pltpu.VMEM((ROUNDS,) + labels.shape, jnp.int32),
             pltpu.VMEM((4, 4, 2, 128, 128), f32),
-            pltpu.VMEM((3, 4, 2, 128, 128), bf16),
-            pltpu.VMEM((2, len(FULL), 2, 128, 128), f32),
-            pltpu.VMEM((3, 4, 2, 128, 128), bf16),
+            pltpu.VMEM((3, 2, 4, 128, 128), bf16),
+            pltpu.VMEM((2, 2, 128, 128), f32),
+            pltpu.VMEM((3, 2, 4, 128, 128), bf16),
             dma((128,)), dma((5 + PARTS,)), dma((PARTS,)), dma((4,)), dma((4, PARTS)), dma((4,)),
-            dma((4,)), dma((2, 4)), dma((7, PARTS + 1)), dma((1,)), dma((3,)), dma((2, len(FULL))), dma((3, 4)), dma((3,)),
+            dma((4,)), dma((2, 4)), dma((7, PARTS + 1)), dma((1,)), dma((3,)), dma((3, 4)), dma((2,)),
         ],
         compiler_params=pltpu.CompilerParams(
             collective_id=0, has_side_effects=True, vmem_limit_bytes=40 * 2**20

time: 69.6 us -> 65.8 us (0.945)
  Pallas kernels: 66.4 us -> 62.2 us
    pallas_call x1, Pallas kernels: 66.4 us -> 62.2 us  [shards(): pl.pallas_call(kernel, out_shape=jax.ShapeDtypeStruct((2, 4, 128, 128), f...]
where the time goes in v4:
time: 65.8 us; the launch traced here: 64.6 us
  Pallas kernels  62.2 us (95%)
  local copies, waits for them, and re-layouts  2.46 us (4%)
    pallas_call x1, Pallas kernels, shards(): pl.pallas_call(kernel, out_shape=jax.ShapeDtypeStruct((2, 4, 128, 128), f...  62.2 us
    unnamed x5, local copies, waits for them, and re-layouts  2.46 us

profile of v4, /device:TPU:6, one launch (start us, length us, event | category | flops | bytes accessed | tf_op | source)
XLA Modules:
  0.0 64.6 jit_solution(643483261988598247)
XLA Ops:
  0.0 0.0 copy-start
  0.0 0.9 %copy-done = bf16[1024,128]{1,0:T(8,128)(2,1)S(1)} copy-done((bf16[1024,128]{1,0:T(8,128)(2,1)S(1)}, bf16[1024,128]{1,0:T(8,128)(2,1)}, u32[]{:S(2)}) %copy-start) | copy-done | bytes 262168
  1.0 0.0 copy-start.1
  1.0 0.7 %copy-done.1 = s32[3,1024]{1,0:T(4,128)S(1)} copy-done((s32[3,1024]{1,0:T(4,128)S(1)}, s32[3,1024]{1,0:T(4,128)}, u32[]{:S(2)}) %copy-start.1) | copy-done | bytes 12312
  1.7 62.2 %shard_map.28 = f32[2,4,128,128]{3,2,1,0:T(8,128)S(1)} custom-call(bf16[4,4,64,128]{3,2,1,0:T(8,128)(2,1)S(1)} %bitcast.3, s32[3,1024]{1,0:T(4,128)S(1)} %copy-done.1), custom_call_target="tpu_custom_call" | custom-call | tf_op jit(solution)/shard_map/pallas_call | solution.py:327
  63.8 0.8 %copy.4 = f32[1024,128]{1,0:T(8,128)} copy(f32[1024,128]{1,0:T(8,128)S(1)} %bitcast.2) | data formatting | bytes 1048576
Async XLA Ops:
  0.0 0.9 %copy-start = (bf16[1024,128]{1,0:T(8,128)(2,1)S(1)}, bf16[1024,128]{1,0:T(8,128)(2,1)}, u32[]{:S(2)}) copy-start(bf16[1024,128]{1,0:T(8,128)(2,1)} %param.2) | copy-start | bytes 786436
  1.0 0.7 %copy-start.1 = (s32[3,1024]{1,0:T(4,128)S(1)}, s32[3,1024]{1,0:T(4,128)}, u32[]{:S(2)}) copy-start(s32[3,1024]{1,0:T(4,128)} %lab_hbm.1) | copy-start | bytes 36868

commit v5 on v4

--- a/solution.py
+++ b/solution.py
@@ -9,9 +9,11 @@
 OWN = 3
 SLOTS = (0, 1, 2, 4, 5, 6)
 ROUNDS = 3
-PARTS = 4
-ROWS = 256 // PARTS
-PARCELS = ((1, 0, 1), (1, 1, 3), (0, 0, 3))
+STRIPES, ROWS = 4, 64
+CUTS = ((0, 2), (2, 1), (3, 1))
+PARTS = len(CUTS)
+PARCELS = ((1, 0, 1), (1, 1, 2), (1, 2, 3), (0, 0, 3))
+LAST = len(PARCELS)
 
 
 def kernel(
@@ -87,7 +89,7 @@
     pl.semaphore_wait(barrier, jnp.where(edge, len(greeted) + 3, len(greeted)))
 
     for j in range(PARTS):
-        send(e_ref.at[:, j], far.at[:, j], r_far.at[j], across)
+        send(e_ref.at[:, pl.ds(*CUTS[j])], far.at[:, pl.ds(*CUTS[j])], r_far.at[j], across)
     for o in (2, 1, 3):
         send(e_ref.at[lax.rem(x + o, 4)], q_ref.at[OWN, h, x], r_qa.at[x], beside(o))
     mine_a = place(e_ref.at[x], q_ref.at[OWN, h, x], 0)
@@ -96,7 +98,7 @@
     for o in (2, 1, 3):
         send(e_ref.at[pl.ds(2 * h, 2)], own.at[h, x], r_own.at[x], beside(o))
     own_a = place(e_ref.at[pl.ds(2 * h, 2)], own.at[h, x], 1)
-    late = (3 - 2 * h, pl.ds(PARTS // 2, PARTS // 2))
+    late = (3 - 2 * h, pl.ds(STRIPES // 2, STRIPES // 2))
     for o in (2, 1, 3):
         send(e_ref.at[late], extra.at[h, x], r_ex.at[h, x], beside(o))
     extra_a = place(e_ref.at[late], extra.at[h, x], 3 + PARTS)
@@ -104,7 +106,7 @@
     def piece(slot, half, index):
         if index == 0:
             return q_ref.at[slot, half]
-        return q_ref.at[slot, 1 - half, :, index - 1]
+        return q_ref.at[slot, 1 - half, :, pl.ds(*CUTS[index - 1])]
 
     def leave(way):
         slot = jnp.where(z == 0, 1, 5)
@@ -132,27 +134,28 @@
 
     def relay(index):
         below, above = half_of(-2), half_of(2)
-        arrived(piece(1, below, index), r_z.at[1, index])
-        arrived(piece(5, above, index), r_z.at[5, index])
-        half = jnp.where(c == 1, below, above)
+        half, rest = jnp.where(c == 1, below, above), jnp.where(c == 1, above, below)
         src, dst = 5 - 4 * c, 6 - 6 * c
+        arrived(piece(src, half, index), r_z.at[src, index])
         send(piece(src, half, index), piece(dst, half, index), r_z.at[dst, index], along(2 * c - 1))
-        dst = 2 * c
-        send(piece(1, below, index), piece(dst, below, index), r_z.at[dst, index], twin)
-        dst = 4 + 2 * c
-        send(piece(5, above, index), piece(dst, above, index), r_z.at[dst, index], twin)
+        dst = 4 - 2 * c
+        send(piece(src, half, index), piece(dst, half, index), r_z.at[dst, index], twin)
+        src, dst = 1 + 4 * c, 6 * c
+        arrived(piece(src, rest, index), r_z.at[src, index])
+        send(piece(src, rest, index), piece(dst, rest, index), r_z.at[dst, index], twin)
 
     def fan(j):
-        arrived(far.at[:, j], r_far.at[j])
+        part_of = pl.ds(*CUTS[j])
+        arrived(far.at[:, part_of], r_far.at[j])
         for o in (2, 1, 3):
-            send(far.at[lax.rem(x + o, 4), j], q_ref.at[OWN, 1 - h, x, j], r_qb.at[x, j], beside(o))
-        place(far.at[x, j], q_ref.at[OWN, 1 - h, x, j], 2 + j)
+            send(far.at[lax.rem(x + o, 4), part_of], q_ref.at[OWN, 1 - h, x, part_of], r_qb.at[x, j], beside(o))
+        place(far.at[x, part_of], q_ref.at[OWN, 1 - h, x, part_of], 2 + j)
 
     def fan_arrived(j):
         for o in (1, 2, 3):
             peer = lax.rem(x + o, 4)
-            arrived(q_ref.at[OWN, 1 - h, peer, j], r_qb.at[peer, j])
-        pltpu.make_async_copy(far.at[x, j], q_ref.at[OWN, 1 - h, x, j], local_sem.at[2 + j]).wait()
+            arrived(q_ref.at[OWN, 1 - h, peer, pl.ds(*CUTS[j])], r_qb.at[peer, j])
+        arrived(q_ref.at[OWN, 1 - h, x, pl.ds(*CUTS[j])], local_sem.at[2 + j])
 
     for o in (1, 2, 3):
         peer = lax.rem(x + o, 4)
@@ -161,32 +164,28 @@
     spread(0)
     fan(0)
     fan(1)
-    fan_arrived(0)
-    spread(1)
-    fan(2)
     @pl.when(edge)
     def _():
         leave(2).wait_recv()
         leave(3).start()
 
-    fan(3)
+    fan_arrived(0)
+    spread(1)
+    fan(2)
+    for o in (2, 1, 3):
+        send(far.at[pl.ds(2 * h, 2)], own.at[1 - h, x], r_ob.at[x], beside(o))
+    own_b = place(far.at[pl.ds(2 * h, 2)], own.at[1 - h, x], 2 + PARTS)
+    for o in (2, 1, 3):
+        send(far.at[late], extra.at[1 - h, x], r_ex.at[1 - h, x], beside(o))
+    extra_b = place(far.at[late], extra.at[1 - h, x], 4 + PARTS)
     fan_arrived(1)
     spread(2)
-    for o in (2, 1, 3):
-        send(far.at[pl.ds(2 * h, 2)], own.at[1 - h, x], r_ob.at[x], beside(o))
-    own_b = place(far.at[pl.ds(2 * h, 2)], own.at[1 - h, x], 2 + PARTS)
-    for o in (2, 1, 3):
-        send(far.at[late], extra.at[1 - h, x], r_ex.at[1 - h, x], beside(o))
-    extra_b = place(far.at[late], extra.at[1 - h, x], 4 + PARTS)
     fan_arrived(2)
     spread(3)
-    fan_arrived(3)
-    spread(4)
     relay(1)
+    relay(0)
     relay(2)
-    relay(0)
     relay(3)
-    relay(4)
     for d in (1, 2, 3):
         arrived(lab_in.at[d - 1], r_lab.at[d - 1])
         row = lab_in[d - 1, d - 1 : d, pl.ds(pl.multiple_of(x * 256, 256), 256)]
@@ -260,13 +259,13 @@
                     small[o - 1, k, t] = tile.astype(jnp.bfloat16)
 
     def parcel(o, m):
-        if m < 3:
+        if m < LAST:
             k, first, end = PARCELS[m]
             at = (o - 1, k, pl.ds(first, end - first))
             return small.at[at], got_small.at[at], r_small.at[o - 1, m]
         if o == 2:
-            return small.at[1, :, 3], got_small.at[1, :, 3], r_small.at[1, 3]
-        return part.at[o, 3], got.at[o // 2], r_small.at[o - 1, 3]
+            return small.at[1, :, 3], got_small.at[1, :, 3], r_small.at[1, LAST]
+        return part.at[o, 3], got.at[o // 2], r_small.at[o - 1, LAST]
 
     def give(o, m):
         send(*parcel(o, m), beside(o))
@@ -284,7 +283,7 @@
 
     def finish(m):
         take(m)
-        if m == 3:
+        if m == LAST:
             out_ref[h, 3] = total(3, 0)
             out_ref[1 - h, 3] = total(3, 1)
             return
@@ -307,14 +306,16 @@
     give(3, 0)
     give(1, 1)
     give(3, 1)
-    for m in (2, 3):
+    for m in range(2, LAST + 1):
         for o in (2, 1, 3):
             give(o, m)
     product(0)
-    for m in range(4):
+    for m in range(LAST + 1):
         finish(m)
-    for k, first, end in PARCELS[:2]:
-        arrived(out_ref.at[1 - h, pl.ds(first, end - first)], r_out.at[first])
+    for m in range(LAST):
+        k, first, end = PARCELS[m]
+        if k == 1:
+            arrived(out_ref.at[1 - h, pl.ds(first, end - first)], r_out.at[m])
     for copy in sent:
         copy.wait_send()
     for copy, inside in (leave(0), z != 7), (leave(1), z != 0), (leave(2), edge), (leave(3), edge):
@@ -323,7 +324,7 @@
 
 def shards(embeddings, labels):
     bf16, f32, dma = jnp.bfloat16, jnp.float32, pltpu.SemaphoreType.DMA
-    block = (4, PARTS, ROWS, 128)
+    block = (4, STRIPES, ROWS, 128)
     out = pl.pallas_call(
         kernel,
         out_shape=jax.ShapeDtypeStruct((2, 4, 128, 128), f32),
@@ -336,7 +337,7 @@
             pltpu.VMEM(block, bf16),
             pltpu.VMEM((7, 2) + block, bf16),
             pltpu.VMEM((2, 4, 2) + block[1:], bf16),
-            pltpu.VMEM((2, 4, PARTS // 2) + block[2:], bf16),
+            pltpu.VMEM((2, 4, STRIPES // 2) + block[2:], bf16),
             pltpu.VMEM((7, 640, 256), bf16),
             pltpu.VMEM((ROUNDS + 1, 640, 128), jnp.int32),
             pltpu.VMEM((ROUNDS + 1, 8, 256), jnp.int32),
@@ -346,7 +347,7 @@
             pltpu.VMEM((2, 2, 128, 128), f32),
             pltpu.VMEM((3, 2, 4, 128, 128), bf16),
             dma((128,)), dma((5 + PARTS,)), dma((PARTS,)), dma((4,)), dma((4, PARTS)), dma((4,)),
-            dma((4,)), dma((2, 4)), dma((7, PARTS + 1)), dma((1,)), dma((3,)), dma((3, 4)), dma((2,)),
+            dma((4,)), dma((2, 4)), dma((7, PARTS + 1)), dma((1,)), dma((3,)), dma((3, 6)), dma((4,)),
         ],
         compiler_params=pltpu.CompilerParams(
             collective_id=0, has_side_effects=True, vmem_limit_bytes=40 * 2**20

time: 65.8 us -> 64.8 us (0.985)
  no operation moved by 1% of the time
where the time goes in v5:
time: 64.8 us; the launch traced here: 64.1 us
  Pallas kernels  61.6 us (95%)
  local copies, waits for them, and re-layouts  2.46 us (4%)
    pallas_call x1, Pallas kernels, shards(): pl.pallas_call(kernel, out_shape=jax.ShapeDtypeStruct((2, 4, 128, 128), f...  61.6 us
    unnamed x5, local copies, waits for them, and re-layouts  2.46 us

profile of v5, /device:TPU:6, one launch (start us, length us, event | category | flops | bytes accessed | tf_op | source)
XLA Modules:
  0.0 64.1 jit_solution(3705558902236448116)
XLA Ops:
  0.0 0.0 copy-start
  0.0 0.9 %copy-done = bf16[1024,128]{1,0:T(8,128)(2,1)S(1)} copy-done((bf16[1024,128]{1,0:T(8,128)(2,1)S(1)}, bf16[1024,128]{1,0:T(8,128)(2,1)}, u32[]{:S(2)}) %copy-start) | copy-done | bytes 262168
  1.0 0.0 copy-start.1
  1.0 0.7 %copy-done.1 = s32[3,1024]{1,0:T(4,128)S(1)} copy-done((s32[3,1024]{1,0:T(4,128)S(1)}, s32[3,1024]{1,0:T(4,128)}, u32[]{:S(2)}) %copy-start.1) | copy-done | bytes 12312
  1.7 61.6 %shard_map.28 = f32[2,4,128,128]{3,2,1,0:T(8,128)S(1)} custom-call(bf16[4,4,64,128]{3,2,1,0:T(8,128)(2,1)S(1)} %bitcast.3, s32[3,1024]{1,0:T(4,128)S(1)} %copy-done.1), custom_call_target="tpu_custom_call" | custom-call | tf_op jit(solution)/shard_map/pallas_call | solution.py:328
  63.3 0.8 %copy.4 = f32[1024,128]{1,0:T(8,128)} copy(f32[1024,128]{1,0:T(8,128)S(1)} %bitcast.2) | data formatting | bytes 1048576
Async XLA Ops:
  0.0 0.9 %copy-start = (bf16[1024,128]{1,0:T(8,128)(2,1)S(1)}, bf16[1024,128]{1,0:T(8,128)(2,1)}, u32[]{:S(2)}) copy-start(bf16[1024,128]{1,0:T(8,128)(2,1)} %param.2) | copy-start | bytes 786436
  1.0 0.7 %copy-start.1 = (s32[3,1024]{1,0:T(4,128)S(1)}, s32[3,1024]{1,0:T(4,128)}, u32[]{:S(2)}) copy-start(s32[3,1024]{1,0:T(4,128)} %lab_hbm.1) | copy-start | bytes 36868

commit v6 on v5

--- a/solution.py
+++ b/solution.py
@@ -238,25 +238,27 @@
 
     lax.fori_loop(0, 6, step, 0)
 
-    def product(o):
-        xd = lax.rem(x + o, 4)
-        left = jnp.concatenate([slope[s] for s in SLOTS], axis=1)
+    def store(o, t, k, tile):
+        if o == 0 or (o != 2 and t == 3):
+            part[o, t, k] = tile
+        else:
+            small[o - 1, k, t] = tile.astype(jnp.bfloat16)
+
+    def product(k, steps):
+        rows, half = (384, 1 - h) if k else (640, h)
+        left = jnp.concatenate([slope[s, :rows] for s in SLOTS], axis=1)
         right = jnp.concatenate(
             [
-                jnp.concatenate([q_ref[s, half, xd].reshape(256, 128) for half in (h, 1 - h)], axis=1)
+                jnp.concatenate([q_ref[s, half, lax.rem(x + o, 4)].reshape(256, 128) for o in steps], axis=1)
                 for s in SLOTS
             ],
             axis=0,
         )
         value = jnp.dot(left, right, preferred_element_type=jnp.float32)
-        for t in range(4):
-            for k in range(2):
-                row, column = (t * 128, k * 128) if t < 3 else (384 + k * 128, 0)
-                tile = value[row : row + 128, column : column + 128]
-                if o == 0 or (o != 2 and t == 3):
-                    part[o, t, k] = tile
-                else:
-                    small[o - 1, k, t] = tile.astype(jnp.bfloat16)
+        for at, o in enumerate(steps):
+            for group in range(rows // 128):
+                tile = value[group * 128 : group * 128 + 128, at * 128 : at * 128 + 128]
+                store(o, min(group, 3), k if group < 3 else group - 3, tile)
 
     def parcel(o, m):
         if m < LAST:
@@ -297,19 +299,19 @@
             rows = pl.ds(first, end - first)
             send(part.at[0, rows, 1], out_ref.at[h, rows], r_out.at[m], across)
 
-    product(2)
+    product(1, (2, 1))
     give(2, 0)
-    product(1)
     give(1, 0)
-    give(2, 1)
-    product(3)
+    product(1, (3, 0))
     give(3, 0)
-    give(1, 1)
-    give(3, 1)
-    for m in range(2, LAST + 1):
+    for m in (1, 2):
         for o in (2, 1, 3):
             give(o, m)
-    product(0)
+    product(0, (2, 1))
+    product(0, (3, 0))
+    for m in range(3, LAST + 1):
+        for o in (2, 1, 3):
+            give(o, m)
     for m in range(LAST + 1):
         finish(m)
     for m in range(LAST):

time: 64.8 us -> 63.1 us (0.974)
  Pallas kernels: 61.6 us -> 59.5 us
    pallas_call x1, Pallas kernels: 61.6 us -> 59.5 us  [shards(): pl.pallas_call(kernel, out_shape=jax.ShapeDtypeStruct((2, 4, 128, 128), f...]
where the time goes in v6:
time: 63.1 us; the launch traced here: 62 us
  Pallas kernels  59.5 us (94%)
  local copies, waits for them, and re-layouts  2.46 us (4%)
    pallas_call x1, Pallas kernels, shards(): pl.pallas_call(kernel, out_shape=jax.ShapeDtypeStruct((2, 4, 128, 128), f...  59.5 us
    unnamed x5, local copies, waits for them, and re-layouts  2.46 us

profile of v6, /device:TPU:6, one launch (start us, length us, event | category | flops | bytes accessed | tf_op | source)
XLA Modules:
  0.0 62.0 jit_solution(12545517428734741258)
XLA Ops:
  0.0 0.0 copy-start
  0.0 0.9 %copy-done = bf16[1024,128]{1,0:T(8,128)(2,1)S(1)} copy-done((bf16[1024,128]{1,0:T(8,128)(2,1)S(1)}, bf16[1024,128]{1,0:T(8,128)(2,1)}, u32[]{:S(2)}) %copy-start) | copy-done | bytes 262168
  1.0 0.0 copy-start.1
  1.0 0.7 %copy-done.1 = s32[3,1024]{1,0:T(4,128)S(1)} copy-done((s32[3,1024]{1,0:T(4,128)S(1)}, s32[3,1024]{1,0:T(4,128)}, u32[]{:S(2)}) %copy-start.1) | copy-done | bytes 12312
  1.7 59.5 %shard_map.28 = f32[2,4,128,128]{3,2,1,0:T(8,128)S(1)} custom-call(bf16[4,4,64,128]{3,2,1,0:T(8,128)(2,1)S(1)} %bitcast.3, s32[3,1024]{1,0:T(4,128)S(1)} %copy-done.1), custom_call_target="tpu_custom_call" | custom-call | tf_op jit(solution)/shard_map/pallas_call | solution.py:330
  61.2 0.8 %copy.4 = f32[1024,128]{1,0:T(8,128)} copy(f32[1024,128]{1,0:T(8,128)S(1)} %bitcast.2) | data formatting | bytes 1048576
Async XLA Ops:
  0.0 0.9 %copy-start = (bf16[1024,128]{1,0:T(8,128)(2,1)S(1)}, bf16[1024,128]{1,0:T(8,128)(2,1)}, u32[]{:S(2)}) copy-start(bf16[1024,128]{1,0:T(8,128)(2,1)} %param.2) | copy-start | bytes 786436
  1.0 0.7 %copy-start.1 = (s32[3,1024]{1,0:T(4,128)S(1)}, s32[3,1024]{1,0:T(4,128)}, u32[]{:S(2)}) copy-start(s32[3,1024]{1,0:T(4,128)} %lab_hbm.1) | copy-start | bytes 36868
